TPU v7x, 32 devices: a whole 2x2x4 slice. The times are simulated.
32 devices in a mesh: groups: 2 (over x), seq: 16 (over z, y, core).
Axes of the slice: x: 2, y: 2, z: 4, core: 2. Of those that a mesh axis runs over, the one named last changes fastest.
Arguments:
- projected: bfloat16 [12288, 3072], P(('groups', 'seq')), parts along dimension 0, may hold values from -6 to 6
- conv_weight: float32 [3, 3072], replicated, may hold values from -3 to 3
- doc_lengths: int32 [64], P('groups'), parts along dimension 0, may hold values from 1 to 1536, 4096 in all
- load_starts: int32 [32], P('groups'), parts along dimension 0, may hold values from 0 to 3904, as said below
Outputs:
- layer_out: bfloat16 [12288, 2048], P(('groups', 'seq')), parts along dimension 0
There are 2 independent parts, one for each index of `groups`. A program takes and returns all parts, laid end to end along the dimension named above; an argument that names none is the same for every part. Nothing has to cross between parts.
Inputs may be any that keep to these rules, and one draw needn't show every extreme that they name: load_starts[0] = 0 and load_starts rises; shard r holds the tokens load_starts[r] to load_starts[r + 1] - 1 (the last shard up to 4095), between 128 and 384 of them, and exactly 384 on some shard; load_starts[r] differs from r * 256 by at most 64, and by exactly 64 in each direction for some shard; the last entry is the largest. `doc_lengths`: the lengths sum to 4096.
All inputs are finite; a program needn't handle non-finite values.
Results may differ from a plain program's by a relative error of at most 0.0059.
Values may be sent and summed in bfloat16 or wider, within the bound.
A program may use at most 256 MiB of HBM per device.

v0:
```python
import jax
import jax.numpy as jnp
import numpy as np
from jax import lax
from jax.sharding import PartitionSpec as P

HEADS = 32
FEAT = 16
HEAD_DIM = 64
CAP = 256
TOK_DEV = 384
TAYLOR = 153


highest = lax.Precision.HIGHEST


def shifted_2(block, axis, distance):
    devices = range(lax.axis_size(axis))
    route = [(i - distance, i) for i in devices if i - distance in devices]
    return lax.ppermute(block, axis, route)


def entering(shard, axis, combine, identity):
    count, place = (lax.axis_size(axis), lax.axis_index(axis))
    everything = jax.tree.map(lambda part: lax.all_gather(part, axis), shard)
    start = jax.tree.map(
        lambda part, zero: jnp.broadcast_to(jnp.asarray(zero, part.dtype), part.shape),
        shard,
        identity,
    )

    def lap(k, before):
        reached = k < place
        new = combine(before, jax.tree.map(lambda part: part[k], everything))
        return jax.tree.map(lambda a, b: jnp.where(reached, a, b), new, before)

    return lax.fori_loop(0, count, lap, start)


def taylor_map(features_in):
    feat_width = features_in.shape[-1]
    upper_a, upper_b = np.triu_indices(feat_width)
    pair_scale = np.where(
        upper_a == upper_b, (2.0 * feat_width) ** (-0.5), feat_width ** (-0.5)
    ).astype(np.float32)
    constant_term = jnp.ones(features_in.shape[:-1] + (1,), features_in.dtype)
    second = features_in[..., upper_a] * features_in[..., upper_b] * pair_scale
    return jnp.concatenate([constant_term, features_in * feat_width ** (-0.25), second], axis=-1)


def doc_start_of(row_ranks, doc_starts):
    inside = doc_starts[None, :] <= row_ranks[:, None]
    return jnp.max(jnp.where(inside, doc_starts[None, :], -1), axis=1)


def convolve(source_rows, count, first_rank, conv_weight, doc_starts):
    rim_width = conv_weight.shape[0] - 1
    tail_rows = lax.dynamic_slice_in_dim(source_rows, count - rim_width, rim_width, 0)
    before = shifted_2(tail_rows, "seq", 1)
    extended = jnp.concatenate([before, source_rows], axis=0).astype(jnp.float32)
    length = source_rows.shape[0]
    row_ranks = first_rank + jnp.arange(length, dtype=jnp.int32)
    row_starts = doc_start_of(row_ranks, doc_starts)
    summed = jnp.zeros(source_rows.shape, jnp.float32)
    for offset in range(conv_weight.shape[0]):
        inside_doc = (row_ranks - offset >= row_starts)[:, None]
        shifted = extended[rim_width - offset : rim_width - offset + length]
        summed = summed + jnp.where(inside_doc, shifted * conv_weight[offset][None, :], 0.0)
    return summed.astype(jnp.bfloat16)


def attend(mixed, row_ranks, valid, first_rank, doc_starts):
    length = mixed.shape[0]
    key_cols = HEADS * FEAT
    queries = mixed[:, :key_cols].reshape(length, HEADS, FEAT)
    key_rows = mixed[:, key_cols : 2 * key_cols].reshape(length, HEADS, FEAT)
    value_rows = mixed[:, 2 * key_cols :].reshape(length, HEADS, HEAD_DIM)
    row_starts = doc_start_of(row_ranks, doc_starts)
    same_doc = (
        valid[:, None]
        & valid[None, :]
        & (row_ranks[None, :] <= row_ranks[:, None])
        & (row_starts[None, :] == row_starts[:, None])
    )
    score_scale = FEAT ** (-0.5)

    def head_terms(operands):
        query_head, key_head, value_head = operands
        scores = jnp.dot(query_head, key_head.T, preferred_element_type=jnp.float32) * score_scale
        weights = jnp.where(same_doc, 1.0 + scores + 0.5 * scores * scores, 0.0)
        numerator = jnp.dot(weights, value_head.astype(jnp.float32), precision=highest)
        return (numerator, jnp.sum(weights, axis=1))

    numerator, denominator = lax.map(
        head_terms,
        (queries.transpose(1, 0, 2), key_rows.transpose(1, 0, 2), value_rows.transpose(1, 0, 2)),
    )
    query_features = taylor_map(queries.astype(jnp.float32))
    key_features = taylor_map(key_rows.astype(jnp.float32))
    last_start = jnp.max(jnp.where(valid, row_starts, -1))
    in_tail = (valid & (row_starts == last_start)).astype(jnp.float32)
    has_start = (last_start >= first_rank).astype(jnp.float32)
    tail_keys = key_features * in_tail[:, None, None]
    local_state = jnp.einsum(
        "rhf,rhe->fhe", tail_keys, value_rows.astype(jnp.float32), precision=highest
    ).reshape(TAYLOR, HEADS * HEAD_DIM)
    local_norm = jnp.sum(tail_keys, axis=0).T

    def combine(earlier, later):
        keep_share = 1.0 - later[0]
        return (
            jnp.maximum(earlier[0], later[0]),
            earlier[1] * keep_share + later[1],
            earlier[2] * keep_share + later[2],
        )

    identity = (jnp.zeros((), jnp.float32), jnp.zeros_like(local_state), jnp.zeros_like(local_norm))
    carried = entering((has_start, local_state, local_norm), "seq", combine, identity)
    from_prior = (valid & (row_starts < first_rank)).astype(jnp.float32)
    prior_state = carried[1].reshape(TAYLOR, HEADS, HEAD_DIM)
    cross_num = jnp.einsum("rhf,fhe->hre", query_features, prior_state, precision=highest)
    cross_den = jnp.einsum("rhf,fh->hr", query_features, carried[2], precision=highest)
    numerator = numerator + from_prior[None, :, None] * cross_num
    denominator = denominator + from_prior[None, :] * cross_den
    divisor = jnp.where(valid[None, :], denominator, 1.0)
    result = jnp.where(valid[None, :, None], numerator / divisor[:, :, None], 0.0)
    return result.transpose(1, 0, 2).reshape(length, HEADS * HEAD_DIM).astype(jnp.bfloat16)


def per_device(projected, conv_weight, doc_lengths, load_starts):
    devices = lax.axis_size("seq")
    shard_index = lax.axis_index("seq")
    doc_starts = jnp.cumsum(doc_lengths) - doc_lengths
    own_start = load_starts[shard_index]
    later_index = jnp.minimum(shard_index + 1, devices - 1)
    next_start = jnp.where(shard_index + 1 < devices, load_starts[later_index], devices * CAP)
    own_count = next_start - own_start
    arrive_slots = jnp.arange(TOK_DEV, dtype=jnp.int32)
    arrive_ranks = own_start + arrive_slots
    arrive_valid = arrive_slots < own_count
    mixed = convolve(projected, own_count, own_start, conv_weight, doc_starts)
    return attend(mixed, arrive_ranks, arrive_valid, own_start, doc_starts)


def solution(mesh):
    return jax.shard_map(
        per_device,
        mesh=mesh,
        in_specs=(P(("groups", "seq"), None), P(), P("groups"), P("groups")),
        out_specs=P(("groups", "seq"), None),
        check_vma=False,
    )
```

profile of v0, /device:TPU:0, one launch (start us, length us, event | category | flops | bytes accessed | tf_op | source)
XLA Modules:
  0.0 365.6 jit_solution(7012839928434791411)
XLA Ops:
  10.2 2.4 collective-permute-start
  15.6 1.9 and_convert_fusion.1
  20.4 2.3 maximum_convert_fusion
  22.7 2.9 fusion.23
  26.7 3.8 %gather_fusion = f32[136,384,32]{1,2,0:T(8,128)} fusion(f32[384,32,16]{0,1,2:T(8,128)S(1)} %copy.61, s32[1024]{0:T(1024)S(1)} %pad_clamp_fusion.1), kind=kCustom, calls=%fused_computation | custom fusion | bytes 13369888 | tf_op jit(solution)/shard_map/gather | solution.py:48
  30.5 3.7 %gather_fusion.1 = f32[136,384,32]{1,2,0:T(8,128)} fusion(f32[384,32,16]{0,1,2:T(8,128)S(1)} %copy.61, s32[1024]{0:T(1024)S(1)} %pad_clamp_fusion), kind=kCustom, calls=%fused_computation.1 | custom fusion | bytes 13369888 | tf_op jit(solution)/shard_map/gather | solution.py:48
  34.3 1.9 copy.58
  37.3 3.7 %gather_fusion.2 = f32[136,384,32]{1,2,0:T(8,128)} fusion(f32[384,32,16]{0,1,2:T(8,128)S(1)} %copy.65, s32[1024]{0:T(1024)S(1)} %pad_clamp_fusion.1), kind=kCustom, calls=%fused_computation.2 | custom fusion | bytes 13369888 | tf_op jit(solution)/shard_map/gather | solution.py:48
  41.0 3.7 %gather_fusion.3 = f32[136,384,32]{1,2,0:T(8,128)} fusion(f32[384,32,16]{0,1,2:T(8,128)S(1)} %copy.65, s32[1024]{0:T(1024)S(1)} %pad_clamp_fusion), kind=kCustom, calls=%fused_computation.3 | custom fusion | bytes 13369888 | tf_op jit(solution)/shard_map/gather | solution.py:48
  47.2 1.9 copy.59
  49.1 21.1 %fusion.16 = (f32[384,32,136]{0,2,1:T(8,128)}, f32[384,32,136]{0,2,1:T(8,128)S(1)}) fusion(f32[136,384,32]{1,2,0:T(8,128)} %gather_fusion.1, f32[136,384,32]{1,2,0:T(8,128)} %gather_fusion, f32[136]{0:T(256)S(1)} %copy-done.11, f32[136,384,32]{1,2,0:T(8,128)} %gather_fusion.3, f32[136,384,32]{1,2,0:T(8,128)} %gather_fusion.2), kind=kLoop, calls=%fused_computation.28 | loop fusion | flops 6684672 | bytes 40108576 | tf_op jit(solution)/shard_map/mul | solution.py:48
  70.2 7.8 %fusion.20 = f32[32,64,153]{2,1,0:T(8,128)} fusion(bf16[384,32,64]{0,2,1:T(8,128)(2,1)S(1)} %bitcast.101, f32[384,32,136]{0,2,1:T(8,128)S(1)} %get-tuple-element.366, f32[384,32,16]{0,2,1:T(8,128)S(1)} %broadcast_multiply_fusion, f32[153]{0:T(256)S(1)} %copy-done.9, f32[384]{0:T(512)S(1)} %copy-done.6), kind=kOutput, calls=%fused_computation.32 | convolution fusion | flops 1449529344 | bytes 10299492 | tf_op jit(solution)/shard_map/rhf,rhe->fhe/dot_general | solution.py:105
  78.0 2.8 copy.69
  83.6 34.7 %all-reduce = f32[16]{0:T(128)S(1)} all-reduce(f32[16]{0:T(128)S(1)} %dynamic-update-slice), channel_id=1, replica_groups=mesh['groups'=2,'seq'=16] {'seq'}, use_global_device_ids=true, to_apply=%add | all-reduce | flops 16 | bytes 128
  118.3 3.9 %fusion.19 = f32[32,153]{1,0:T(8,128)S(1)} fusion(f32[384,32,136]{0,2,1:T(8,128)} %copy-done, f32[384,32,16]{0,2,1:T(8,128)S(1)} %copy-done.2, f32[153]{0:T(256)S(1)} %copy-done.9, f32[384]{0:T(512)S(1)} %copy-done.6), kind=kLoop, calls=%fused_computation.31 | loop fusion | flops 7515360 | bytes 7492836 | tf_op jit(solution)/shard_map/reduce_sum | solution.py:108
  122.2 21.7 %all-gather.1 = f32[16,153,32]{1,2,0:T(8,128)S(1)} all-gather(f32[1,153,32]{1,2,0:T(8,128)S(1)} %bitcast.106), channel_id=2, replica_groups=mesh['groups'=2,'seq'=16] {'seq'}, dimensions={0}, use_global_device_ids=true | all-gather | bytes 332928 | tf_op jit(solution)/shard_map/all_gather | solution.py:26
  144.9 137.2 %while.33 = (s32[]{:T(128)}, f32[32,384,64]{1,2,0:T(8,128)}, f32[32,384]{1,0:T(8,128)}, bf16[32,384,16]{1,2,0:T(8,128)(2,1)S(1)}, bf16[32,384,16]{1,2,0:T(8,128)...) while((s32[]{:T(128)}, f32[32,384,64]{1,2,0:T(8,128)}, ...), condition=%wide.region_4.5_spmd.clone.clone, body=%wide.region_2.4_spmd.clone.sunk.clone | while | flops 119733888 | bytes 1370721 | solution.py:95
  146.1 1.8 fusion.60
  150.4 1.8 fusion.60
  154.7 1.8 fusion.60
  163.2 1.8 fusion.60
  167.5 1.8 fusion.60
  171.8 1.8 fusion.60
  176.1 1.8 fusion.60
  180.4 1.8 fusion.60
  193.2 1.8 fusion.60
  197.5 1.8 fusion.60
  201.8 1.8 fusion.60
  206.1 1.8 fusion.60
  210.3 1.8 fusion.60
  214.6 1.8 fusion.60
  218.9 1.8 fusion.60
  223.2 1.8 fusion.60
  227.5 1.8 fusion.60
  231.8 1.8 fusion.60
  240.4 1.8 fusion.60
  248.9 1.8 fusion.60
  253.2 1.8 fusion.60
  257.5 1.8 fusion.60
  261.8 1.8 fusion.60
  266.1 1.8 fusion.60
  270.4 1.8 fusion.60
  274.7 1.8 fusion.60
  279.0 1.8 fusion.60
  282.6 52.6 %while.34 = (s32[]{:T(128)}, f32[153,2048]{1,0:T(8,128)S(1)}, f32[153,32]{1,0:T(8,128)S(1)}, s32[]{:T(128)}, f32[16]{0:T(128)S(1)}, /*index=5*/f32[16,153,2048]{2,1,0:T(8,128)}, f32[16,153,32]{1,2,0:T(8,128)S(1)}, f32[1]{0:T(128)}) while((s32[]{:T(128)}, f32[153,2048]{1,0:T(8,128)S(1)}, f32[153,32]{1,0:T(8,128)S(1)}, ...), condition=%wide.region_8.9_spmd.clone.clone, body=%wide.region_7.8_spmd.clone.sunk.clone | while | flops 1272965 | bytes 3897363 | solution.py:38
  283.7 2.0 fusion.61
  287.0 2.0 fusion.61
  290.3 2.0 fusion.61
  293.6 2.0 fusion.61
  296.9 2.0 fusion.61
  300.2 2.0 fusion.61
  303.5 2.0 fusion.61
  306.7 2.0 fusion.61
  310.0 2.0 fusion.61
  313.3 2.0 fusion.61
  316.6 2.0 fusion.61
  319.9 2.0 fusion.61
  323.2 2.0 fusion.61
  326.5 2.0 fusion.61
  329.7 2.0 fusion.61
  333.0 2.0 fusion.61
  336.1 9.2 %fusion.17 = f32[32,1,384]{2,1,0:T(1,128)S(1)} fusion(f32[153,32,1]{0,2,1:T(1,128)S(1)} %copy.73, f32[384,32,136]{0,2,1:T(8,128)} %get-tuple-element.365, f32[384,32,16]{0,2,1:T(8,128)} %broadcast_multiply_fusion.1, f32[153]{0:T(256)S(1)} %copy-done.10), kind=kOutput, calls=%fused_computation.29 | convolution fusion | flops 26320896 | bytes 7540452 | tf_op jit(solution)/shard_map/rhf,fh->hr/dot_general | solution.py:123
  345.3 10.8 %select_convert_fusion = bf16[32,384,64]{1,2,0:T(8,128)(2,1)} fusion(f32[32,384,64]{1,2,0:T(8,128)S(1)} %copy-done.14, f32[153,32,64]{0,2,1:T(8,128)S(1)} %bitcast.103, f32[384,32,136]{0,2,1:T(8,128)} %get-tuple-element.365, f32[384,32,16]{0,2,1:T(8,128)S(1)} %copy-done.4, f32[153]{0:T(256)S(1)} %copy-done.10, f32[32,384]{1,0:T(8,128)S(1)} %fusion.32, ...), kind=kOutput, calls=%fused_computation.46 | convolution fusion | flops 1451581440 | bytes 13494756 | tf_op jit(solution)/shard_map/rhf,fhe->hre/dot_general | solution.py:122
  356.2 2.6 copy.72
  (232 shorter events, 116.5 us)
Async XLA Ops:
  6.5 275.6 %all-gather.4.cloned.1.call-start = ((), (), s32[]{:S(2)}) async-start(), calls=%async_computation | async-start | bytes 22282240 | tf_op jit(solution)/shard_map/all_gather | solution.py:26
  10.2 10.2 %collective-permute-start = (bf16[2,3072]{1,0:T(2,128)(2,1)S(1)}, bf16[2,3072]{1,0:T(2,128)(2,1)S(1)}, u32[]{:S(2)}, u32[]{:S(2)}) collective-permute-start(bf16[2,3072]{1,0:T(2,128)(2,1)S(1)} %constant_dynamic-slice_fusion.1), channel_id=1, source_target_pairs={{0,1},{1,2},{2,3},{3,4},{4,5},{5,6},{6,7},{7,8},{8,9},{9,10},{10,1... | collective-permute-start | bytes 36872 | tf_op jit(solution)/shard_map/ppermute | solution.py:21
  13.3 9.4 %copy-start.7 = (s32[384]{0:T(512)}, s32[384]{0:T(512)S(1)}, u32[]{:S(2)}) copy-start(s32[384]{0:T(512)S(1)} %iota_add_fusion) | copy-start | bytes 4612
  44.7 4.4 %copy-start.11 = (f32[136]{0:T(256)S(1)}, f32[136]{0:T(256)}, u32[]{:S(2)}) copy-start(f32[136]{0:T(256)} %constant.127.clone) | copy-start | bytes 1636
  45.8 24.4 %copy-start.1 = (f32[384,32,16]{0,2,1:T(8,128)}, f32[384,32,16]{0,2,1:T(8,128)S(1)}, u32[]{:S(2)}) copy-start(f32[384,32,16]{0,2,1:T(8,128)S(1)} %broadcast_multiply_fusion) | copy-start | bytes 2359300
  49.0 21.1 %copy-start.3 = (bf16[384,2048]{0,1:T(8,128)(2,1)}, bf16[384,2048]{0,1:T(8,128)(2,1)S(1)}, u32[]{:S(2)}) copy-start(bf16[384,2048]{0,1:T(8,128)(2,1)S(1)} %copy.59) | copy-start | bytes 4718596
  49.1 21.1 %copy-start.6 = (f32[384]{0:T(512)S(1)}, f32[384]{0:T(512)}, u32[]{:S(2)}) copy-start(f32[384]{0:T(512)} %get-tuple-element.361) | copy-start | bytes 4612
  49.1 21.1 %copy-start.9 = (f32[153]{0:T(256)S(1)}, f32[153]{0:T(256)}, u32[]{:S(2)}) copy-start(f32[153]{0:T(256)} %pad.3.clone) | copy-start | bytes 1840
  70.1 7.8 %copy-start = (f32[384,32,136]{0,2,1:T(8,128)}, f32[384,32,136]{0,2,1:T(8,128)S(1)}, u32[]{:S(2)}) copy-start(f32[384,32,136]{0,2,1:T(8,128)S(1)} %get-tuple-element.366) | copy-start | bytes 20054020
  70.2 11.9 %copy-start.15 = (u32[32]{0:T(128)S(1)}, u32[32]{0:T(128)}, u32[]{:S(2)}) copy-start(u32[32]{0:T(128)} %constant.136) | copy-start | bytes 388
  78.0 40.3 %copy-start.2 = (f32[384,32,16]{0,2,1:T(8,128)S(1)}, f32[384,32,16]{0,2,1:T(8,128)}, u32[]{:S(2)}) copy-start(f32[384,32,16]{0,2,1:T(8,128)} %copy-done.1) | copy-start | bytes 2359300
  80.8 64.2 %copy-start.8 = (s32[384]{0:T(512)S(1)}, s32[384]{0:T(512)}, u32[]{:S(2)}) copy-start(s32[384]{0:T(512)} %copy-done.7) | copy-start | bytes 4612
  282.1 0.5 copy-start.12
  282.1 54.0 %copy-start.10 = (f32[153]{0:T(256)S(1)}, f32[153]{0:T(256)}, u32[]{:S(2)}) copy-start(f32[153]{0:T(256)} %pad.3.clone) | copy-start | bytes 1840
  336.1 9.2 %copy-start.5 = (f32[32,384]{1,0:T(8,128)S(1)}, f32[32,384]{1,0:T(8,128)}, u32[]{:S(2)}) copy-start(f32[32,384]{1,0:T(8,128)} %get-tuple-element.222) | copy-start | bytes 147460
  336.1 9.2 %copy-start.13 = (pred[384]{0:T(512)(128)(4,1)S(1)}, pred[384]{0:T(512)(128)(4,1)}, u32[]{:S(2)}) copy-start(pred[384]{0:T(512)(128)(4,1)} %copy-done.12) | copy-start | bytes 1156
  336.1 9.2 %copy-start.4 = (f32[384,32,16]{0,2,1:T(8,128)S(1)}, f32[384,32,16]{0,2,1:T(8,128)}, u32[]{:S(2)}) copy-start(f32[384,32,16]{0,2,1:T(8,128)} %broadcast_multiply_fusion.1) | copy-start | bytes 2359300
  336.1 9.2 %copy-start.14 = (f32[32,384,64]{1,2,0:T(8,128)S(1)}, f32[32,384,64]{1,2,0:T(8,128)}, u32[]{:S(2)}) copy-start(f32[32,384,64]{1,2,0:T(8,128)} %get-tuple-element.220) | copy-start | bytes 9437188
Sparse Core Ops, SparseCore 0:
  80.9 116.6 all-gather.3
where the time goes:
time: 372 us; the launch traced here: 366 us
  matrix products  123 us (33%)
  local copies, waits for them, and re-layouts  88.1 us (24%)
  other arithmetic  69.8 us (19%)
  blocking collectives  56.4 us (15%)
  between operations  16.4 us (4%)
  loops' own time  9.96 us (3%)
    dot_general x32, matrix products, head_terms(): jnp.dot(weights, value_head.astype(jnp.float32), precision=highest)  57.3 us
    dynamic_update_slice x32, local copies, waits for them, and re-layouts, attend(): lax.map(head_terms, (queries.transpose(1, 0, 2), key_rows.transpose(1, 0,...  42.2 us
    dot_general x32, matrix products, head_terms(): jnp.dot(query_head, key_head.T, preferred_element_type=jnp.float32)  37.5 us
    unnamed x1, blocking collectives  34.7 us
    select_n x32, other arithmetic, lap(): return jax.tree.map(lambda a, b: jnp.where(reached, a, b), new, before)  32.1 us
    all_gather x1, blocking collectives, entering(): everything = jax.tree.map(lambda part: lax.all_gather(part, axis), shard)  21.7 us
    mul x1, other arithmetic, taylor_map(): second = features_in[..., upper_a] * features_in[..., upper_b] * pair_scale  21.1 us
    gather x4, local copies, waits for them, and re-layouts, taylor_map(): second = features_in[..., upper_a] * features_in[..., upper_b] * pair_scale  15 us
  transfers between devices with their start and end apart: 2, of which 0 were waited for; matrix products, arithmetic and copies ran while one was open for 41% of the time, Pallas kernels for 0%

commit v1 on v0

v1 whole, which is shorter than its diff:
```python
import functools

import jax
import jax.numpy as jnp
from jax import lax
from jax.experimental import pallas as pl
from jax.experimental.pallas import tpu as pltpu
from jax.sharding import PartitionSpec as P

HEADS = 32
FEAT = 16
HEAD_DIM = 64
CAP = 256
PLANE = 4
KEYS = HEADS * FEAT
PAIRS = HEADS // 2
PER = PAIRS // PLANE
ROWS = 160
MESH = pl.DeviceIdType.MESH
F32 = jnp.float32
BF16 = jnp.bfloat16


def lanes(index, width=128):
    return pl.ds(pl.multiple_of(index * 128, 128), width)


def features(x, one, two):
    parts = [x * x]
    scaled = x * two
    for d in range(1, FEAT // 2):
        parts.append(scaled * pltpu.roll(x, d, 0))
    parts.append(scaled)
    parts.append(scaled[:8] * x[8:])
    row = lax.broadcasted_iota(jnp.int32, (8, x.shape[1]), 0)
    parts.append(jnp.where(row == 0, one, 0.0))
    return jnp.concatenate(parts, axis=0)


def kernel(n, proj, conv_w, doc_len, starts, out, mixed, key_t, query_t, m1, m2, tail,
           prior, valid_cols, causal, tail_rows, halo, local, from_plane, total, from_z,
           carry_out, carried, norm, acc, phi_q, halo_sem, a_send, a_recv, b_send, b_recv,
           c_send, c_recv):
    length = proj.shape[0]
    channels = proj.shape[1]
    me = lax.axis_index("seq")
    z, j = me // PLANE, me % PLANE
    planes = n // PLANE
    base = z * PLANE

    def signal(target):
        pl.semaphore_signal(barrier, inc=1, device_id={"seq": target}, device_id_type=MESH)

    def one_if(cond):
        return jnp.where(cond, 1, 0)

    barrier = pltpu.get_barrier_semaphore()
    for d in range(1, PLANE):
        signal(base + (j + d) % PLANE)
    edges = [
        (z >= 1, me - PLANE), (z >= 2, me - 2 * PLANE),
        (z < planes - 1, me + PLANE), (z < planes - 2, me + 2 * PLANE),
        ((j == PLANE - 1) & (z < planes - 1), me + 1), ((j == 0) & (z >= 1), me - 1),
    ]
    expected = PLANE - 1
    for cond, target in edges:
        pl.when(cond)(functools.partial(signal, target))
        expected = expected + one_if(cond)

    def start_of(r):
        return jnp.where(r < n, starts[jnp.minimum(jnp.maximum(r, 0), n - 1)], n * CAP)

    own = starts[me]
    after = start_of(me + 1)
    count = after - own
    edge = [start_of(base + i) for i in range(-PLANE, PLANE + 1)]

    row16 = lax.broadcasted_iota(jnp.int32, (16, channels), 0)
    token = lax.broadcasted_iota(jnp.int32, (16, length), 1)
    order = lax.broadcasted_iota(jnp.int32, (16, length), 0)
    last_two = (token == count - 2 + order) & (order < 2)
    pick_last = jnp.where(last_two, 1.0, 0.0).astype(BF16)

    def pick(tile, _):
        at = lanes(tile * 4, 512)
        tail_rows[:, at] = jnp.dot(
            pick_last, proj[:, at], preferred_element_type=F32).astype(BF16)
        return 0

    lax.fori_loop(0, channels // 512, pick, 0)

    pl.semaphore_wait(barrier, expected)
    halo_copy = pltpu.make_async_remote_copy(
        src_ref=tail_rows, dst_ref=halo, send_sem=halo_sem.at[0], recv_sem=halo_sem.at[1],
        device_id={"seq": me + 1}, device_id_type=MESH)
    pl.when(me < n - 1)(halo_copy.start)

    @pl.when(me == 0)
    def _():
        halo[...] = jnp.zeros_like(halo)

    @pl.when(z < 1)
    def _():
        from_z[0] = jnp.zeros_like(from_z[0])

    @pl.when(z < 2)
    def _():
        from_z[1] = jnp.zeros_like(from_z[1])

    slot_row = lax.broadcasted_iota(jnp.int32, (8, length), 1)
    rank_row = slot_row + own

    def doc(i, state):
        begin, row_start, last, opens = state
        row_start = jnp.where(begin <= rank_row, begin, row_start)
        last = jnp.where(begin < after, begin, last)
        opens = tuple(
            jnp.where(begin < edge[k + PLANE], begin, o) for k, o in enumerate(opens))
        return begin + doc_len[i], row_start, last, opens

    zero = jnp.int32(0)
    _, row_start, last, opens = lax.fori_loop(
        0, doc_len.shape[0], doc,
        (zero, jnp.zeros((8, length), jnp.int32), zero, (zero,) * (PLANE + 1)))
    start_row = row_start.astype(F32)[:1]
    start_col = jnp.broadcast_to(start_row, (128, length)).T
    slot_col = lax.broadcasted_iota(jnp.int32, (length, 128), 0)
    rank_col = (slot_col + own).astype(F32)
    valid_col = slot_col < count
    m1[...] = jnp.where(rank_col - 1.0 >= start_col, 1.0, 0.0)
    m2[...] = jnp.where(rank_col - 2.0 >= start_col, 1.0, 0.0)
    tail[...] = jnp.where(valid_col & (start_col == last.astype(F32)), 1.0, 0.0).astype(BF16)
    valid_row = slot_row < count
    prior[...] = jnp.where(valid_row & (row_start < own), 1.0, 0.0)
    for i in range(length // 128):
        part = slice(i * 128, i * 128 + 128)
        u = lax.broadcasted_iota(jnp.int32, (length, 128), 1) + i * 128
        same = (start_col == start_row[:, part]) & (u <= slot_col) & valid_col
        causal[:, part] = jnp.where(same, 1.0, 0.0).astype(BF16)

    def conv(tile, _):
        at = lanes(tile)
        x = proj[:, at].astype(F32)
        total_ = x * conv_w[0:1, at]
        total_ = total_ + pltpu.roll(x, 1, 0) * conv_w[1:2, at] * m1[...]
        total_ = total_ + pltpu.roll(x, 2, 0) * conv_w[2:3, at] * m2[...]
        mixed[:, at] = total_.astype(BF16)
        return 0

    def conv_edge():
        x = proj[0:16, :].astype(F32)
        before = halo[...].astype(F32)
        x1 = jnp.where(row16 < 1, pltpu.roll(before, 15, 0), pltpu.roll(x, 1, 0))
        x2 = jnp.where(row16 < 2, before, pltpu.roll(x, 2, 0))
        total_ = x * conv_w[0:1, :]
        total_ = total_ + x1 * conv_w[1:2, :] * m1[0:16, :1]
        total_ = total_ + x2 * conv_w[2:3, :] * m2[0:16, :1]
        mixed[0:16, :] = total_.astype(BF16)

    lax.fori_loop(0, channels // 128, conv, 0)
    pl.when(me > 0)(halo_copy.wait_recv)
    conv_edge()

    def turn_keys(tile, _):
        at = lanes(tile + KEYS // 128)
        key_t[lanes(tile), :] = mixed[:, at].astype(F32).T
        return 0

    lax.fori_loop(0, KEYS // 128, turn_keys, 0)

    lane = lax.broadcasted_iota(jnp.int32, (1, 128), 1)
    low = lane < 64

    def values_at(pair):
        return mixed[:, lanes(pair + 2 * KEYS // 128)]

    def state_pair(d, chunk, pp):
        pair = chunk * PER + pp
        v = values_at(pair) * tail[...]
        keys = key_t[pl.ds(pl.multiple_of(pair * 32, 32), 32), :]
        s_even = jnp.dot(features(keys[:16], 1.0, 1.0).astype(BF16),
                         jnp.where(low, v, tail[...]), preferred_element_type=F32)
        s_odd = jnp.dot(features(keys[16:], 1.0, 1.0).astype(BF16),
                        jnp.where(low, tail[...], v), preferred_element_type=F32)
        local[d, :, lanes(pp)] = jnp.where(low, s_even, s_odd).astype(BF16)
        norm[...] = jnp.where(lane == pp + 64, s_even, jnp.where(lane == pp, s_odd, norm[...]))

    a_copies = {}
    for d in (1, 2, 3, 0):
        chunk = (j + d) % PLANE
        norm[...] = jnp.zeros_like(norm)

        def step(pp, _, d=d, chunk=chunk):
            state_pair(d, chunk, pp)
            return 0

        lax.fori_loop(0, PER, step, 0)
        local[d, :, PER * 128:] = norm[...].astype(BF16)
        if d:
            a_copies[d] = pltpu.make_async_remote_copy(
                src_ref=local.at[d], dst_ref=from_plane.at[d], send_sem=a_send.at[d],
                recv_sem=a_recv.at[d], device_id={"seq": base + chunk}, device_id_type=MESH)
            a_copies[d].start()

    def turn_queries(tile, _):
        at = lanes(tile)
        scaled = mixed[:, at].astype(F32) * 0.25
        mixed[:, at] = scaled.astype(BF16)
        query_t[at, :] = scaled.T
        return 0

    lax.fori_loop(0, KEYS // 128, turn_queries, 0)

    def query_features(head, _):
        q = query_t[pl.ds(pl.multiple_of(head * 16, 16), 16), :]
        phi = features(q, 2.0, 2.0) * prior[0:1, :]
        phi = jnp.concatenate([phi, jnp.zeros((256 - ROWS, length), F32)], axis=0)
        phi_q[head] = phi.astype(BF16).T
        return 0

    lax.fori_loop(0, HEADS // 2, query_features, 0)

    def gathered(d):
        return local[0] if d == 0 else from_plane[d]

    for d in range(1, PLANE):
        a_copies[d].wait_recv()
    total_sum = jnp.zeros(total.shape, F32)
    for d in range(PLANE):
        source = (j - d + PLANE) % PLANE
        keep = jnp.where(opens[PLANE] < start_of(base + source + 1), 1.0, 0.0)
        total_sum = total_sum + gathered(d).astype(F32) * keep
    total[...] = total_sum.astype(BF16)
    b_copies = []
    for k in (1, 2):
        b_copies.append(pltpu.make_async_remote_copy(
            src_ref=total, dst_ref=from_z.at[k - 1], send_sem=b_send.at[k - 1],
            recv_sem=b_recv.at[k - 1], device_id={"seq": me + k * PLANE}, device_id_type=MESH))
        pl.when(z < planes - k)(b_copies[-1].start)

    lax.fori_loop(HEADS // 2, HEADS, query_features, 0)

    key_row = lax.broadcasted_iota(jnp.int32, (128, 1), 0) // FEAT
    half = 256
    def attend(pair, _):
        tile = pair // 4
        v = values_at(pair)
        q = mixed[:, lanes(tile)]
        keys = key_t[lanes(tile), :]
        one = jnp.ones_like(v)
        for side in range(2):
            here = (pair % 4) * 2 + side
            k = jnp.where(key_row == here, keys, 0.0).astype(BF16)
            va = jnp.where(low, v, one) if side == 0 else jnp.where(low, one, v)
            for lo, hi in ((0, half), (half, length)):
                s = jnp.dot(q[lo:hi], k[:, :hi], preferred_element_type=F32) + 1.0
                w = (s * s + 1.0).astype(BF16) * causal[lo:hi, :hi]
                acc[pair * 2 + side, lo:hi, :] = jnp.dot(
                    w, va[:hi], preferred_element_type=F32)
        return 0

    lax.fori_loop(0, PAIRS * 5 // 8, attend, 0)

    for k in (1, 2):
        pl.when(z >= k)(b_copies[k - 1].wait_recv)
    c_copies = {}
    for d in (1, 2, 3, 0):
        to = (j + d) % PLANE
        open_at = opens[0]
        for i in range(1, PLANE):
            open_at = jnp.where(to == i, opens[i], open_at)
        state = from_z[0].astype(F32) * jnp.where(open_at < edge[PLANE], 1.0, 0.0)
        state = state + from_z[1].astype(F32) * jnp.where(open_at < edge[0], 1.0, 0.0)
        for e in range(PLANE):
            source = (j - e + PLANE) % PLANE
            keep = (source < to) & (open_at < start_of(base + source + 1))
            state = state + gathered(e).astype(F32) * jnp.where(keep, 1.0, 0.0)
        if d:
            carry_out[d] = state.astype(BF16)
            c_copies[d] = pltpu.make_async_remote_copy(
                src_ref=carry_out.at[d], dst_ref=carried.at[d], send_sem=c_send.at[d],
                recv_sem=c_recv.at[d], device_id={"seq": base + to}, device_id_type=MESH)
            c_copies[d].start()
        else:
            carried[0] = state.astype(BF16)

    lax.fori_loop(PAIRS * 5 // 8, PAIRS, attend, 0)

    from_row = lax.broadcasted_iota(jnp.int32, (128, 256), 0)
    to_col = lax.broadcasted_iota(jnp.int32, (128, 256), 1)
    pad = jnp.zeros((256 - ROWS, 128), BF16)
    for d in range(PLANE):
        if d:
            c_copies[d].wait_recv()
        chunk = (j - d + PLANE) % PLANE

        def finish(pp, _, d=d, chunk=chunk):
            pair = chunk * PER + pp
            values = carried[d, :, lanes(pp)]
            pick = ((from_row == pp + 64) & (to_col < 128)) | ((from_row == pp) & (to_col >= 128))
            norms = jnp.dot(carried[d, :, PER * 128:], jnp.where(pick, 1.0, 0.0).astype(BF16),
                            preferred_element_type=F32).astype(BF16)
            s_even = jnp.concatenate([jnp.where(low, values, norms[:, :128]), pad], axis=0)
            s_odd = jnp.concatenate([jnp.where(low, norms[:, 128:], values), pad], axis=0)
            even = acc[pair * 2] + jnp.dot(phi_q[pair * 2], s_even, preferred_element_type=F32)
            odd = acc[pair * 2 + 1] + jnp.dot(phi_q[pair * 2 + 1], s_odd, preferred_element_type=F32)
            numer = jnp.where(low, even, odd)
            denom = pltpu.roll(jnp.where(low, odd, even), 64, 1)
            good = denom != 0.0
            result = jnp.where(good, numer / jnp.where(good, denom, 1.0), 0.0)
            out[:, lanes(pair)] = result.astype(BF16)
            return 0

        lax.fori_loop(0, PER, finish, 0)

    pl.when(me < n - 1)(halo_copy.wait_send)
    for d in range(1, PLANE):
        a_copies[d].wait_send()
        c_copies[d].wait_send()
    for k in (1, 2):
        pl.when(z < planes - k)(b_copies[k - 1].wait_send)


def per_device(projected, conv_weight, doc_lengths, load_starts):
    n = lax.axis_size("seq")
    length, channels = projected.shape
    state = (ROWS, (PER + 1) * 128)
    vmem = pl.BlockSpec(memory_space=pltpu.VMEM)
    smem = pl.BlockSpec(memory_space=pltpu.SMEM)
    return pl.pallas_call(
        functools.partial(kernel, n),
        out_shape=jax.ShapeDtypeStruct((length, HEADS * HEAD_DIM), BF16),
        in_specs=[vmem, vmem, smem, smem],
        out_specs=vmem,
        scratch_shapes=[
            pltpu.VMEM((length, channels), BF16),
            pltpu.VMEM((KEYS, length), F32),
            pltpu.VMEM((KEYS, length), F32),
            pltpu.VMEM((length, 128), F32),
            pltpu.VMEM((length, 128), F32),
            pltpu.VMEM((length, 128), BF16),
            pltpu.VMEM((8, length), F32),
            pltpu.VMEM((8, 128), F32),
            pltpu.VMEM((length, length), BF16),
            pltpu.VMEM((16, channels), BF16),
            pltpu.VMEM((16, channels), BF16),
            pltpu.VMEM((PLANE,) + state, BF16),
            pltpu.VMEM((PLANE,) + state, BF16),
            pltpu.VMEM(state, BF16),
            pltpu.VMEM((2,) + state, BF16),
            pltpu.VMEM((PLANE,) + state, BF16),
            pltpu.VMEM((PLANE,) + state, BF16),
            pltpu.VMEM((ROWS, 128), F32),
            pltpu.VMEM((HEADS, length, 128), F32),
            pltpu.VMEM((HEADS, length, 256), BF16),
            pltpu.SemaphoreType.DMA((2,)),
            pltpu.SemaphoreType.DMA((PLANE,)),
            pltpu.SemaphoreType.DMA((PLANE,)),
            pltpu.SemaphoreType.DMA((2,)),
            pltpu.SemaphoreType.DMA((2,)),
            pltpu.SemaphoreType.DMA((PLANE,)),
            pltpu.SemaphoreType.DMA((PLANE,)),
        ],
        compiler_params=pltpu.CompilerParams(
            collective_id=0, has_side_effects=True, vmem_limit_bytes=48 * 1024 * 1024),
    )(projected, conv_weight, doc_lengths, load_starts)


def solution(mesh):
    return jax.shard_map(
        per_device,
        mesh=mesh,
        in_specs=(P(("groups", "seq"), None), P(), P("groups"), P("groups")),
        out_specs=P(("groups", "seq"), None),
        check_vma=False,
    )
```

time: 372 us -> 50.1 us (0.13)
  the two profiles are of different devices: /device:TPU:0 before, /device:TPU:27 now
where the time goes in v1:
time: 50.1 us; the launch traced here: 49.8 us
  Pallas kernels  44.9 us (90%)
  local copies, waits for them, and re-layouts  4.92 us (10%)
    pallas_call x1, Pallas kernels, per_device(): pl.pallas_call(functools.partial(kernel, n), out_shape=jax.ShapeDtypeStru...  44.9 us
    unnamed x9, local copies, waits for them, and re-layouts  4.92 us

profile of v1, /device:TPU:27, one launch (start us, length us, event | category | flops | bytes accessed | tf_op | source)
XLA Modules:
  0.0 49.8 jit_solution(529569515230091542)
XLA Ops:
  0.0 0.0 copy-start
  0.0 1.7 %copy-done = bf16[384,3072]{1,0:T(8,128)(2,1)S(1)} copy-done((bf16[384,3072]{1,0:T(8,128)(2,1)S(1)}, bf16[384,3072]{1,0:T(8,128)(2,1)}, u32[]{:S(2)}) %copy-start) | copy-done | bytes 2359320
  1.7 0.0 copy-start.1
  1.7 0.8 %copy-done.1 = f32[3,3072]{1,0:T(4,128)S(1)} copy-done((f32[3,3072]{1,0:T(4,128)S(1)}, f32[3,3072]{1,0:T(4,128)}, u32[]{:S(2)}) %copy-start.1) | copy-done | bytes 36888
  2.5 0.0 copy-start.2
  2.5 0.7 %copy-done.2 = s32[32]{0:T(128)S(1)} copy-done((s32[32]{0:T(128)S(1)}, s32[32]{0:T(128)}, u32[]{:S(2)}) %copy-start.2) | copy-done | bytes 152
  3.1 0.0 copy-start.3
  3.1 0.7 %copy-done.3 = s32[16]{0:T(128)S(1)} copy-done((s32[16]{0:T(128)S(1)}, s32[16]{0:T(128)}, u32[]{:S(2)}) %copy-start.3) | copy-done | bytes 88
  3.8 44.9 %shard_map.46 = bf16[384,2048]{1,0:T(8,128)(2,1)S(1)} custom-call(bf16[384,3072]{1,0:T(8,128)(2,1)S(1)} %copy-done, f32[3,3072]{1,0:T(4,128)S(1)} %copy-done.1, s32[32]{0:T(128)S(1)} %copy-done.2, s32[16]{0:T(128)S(1)} %copy-done.3), custom_call_target="tpu_custom_call" | custom-call | tf_op jit(solution)/shard_map/pallas_call | solution.py:330
  48.7 1.1 %copy.6 = bf16[384,2048]{1,0:T(8,128)(2,1)} copy(bf16[384,2048]{1,0:T(8,128)(2,1)S(1)} %shard_map.46) | data formatting | bytes 3145728
Async XLA Ops:
  0.0 1.7 %copy-start = (bf16[384,3072]{1,0:T(8,128)(2,1)S(1)}, bf16[384,3072]{1,0:T(8,128)(2,1)}, u32[]{:S(2)}) copy-start(bf16[384,3072]{1,0:T(8,128)(2,1)} %proj.1) | copy-start | bytes 7077892
  1.7 0.8 %copy-start.1 = (f32[3,3072]{1,0:T(4,128)S(1)}, f32[3,3072]{1,0:T(4,128)}, u32[]{:S(2)}) copy-start(f32[3,3072]{1,0:T(4,128)} %conv_w.1) | copy-start | bytes 110596
  2.5 0.7 %copy-start.2 = (s32[32]{0:T(128)S(1)}, s32[32]{0:T(128)}, u32[]{:S(2)}) copy-start(s32[32]{0:T(128)} %doc_len.1) | copy-start | bytes 388
  3.1 0.7 %copy-start.3 = (s32[16]{0:T(128)S(1)}, s32[16]{0:T(128)}, u32[]{:S(2)}) copy-start(s32[16]{0:T(128)} %starts.1) | copy-start | bytes 196

commit v2 on v1

--- a/solution.py
+++ b/solution.py
@@ -37,10 +37,14 @@
     return jnp.concatenate(parts, axis=0)
 
 
-def kernel(n, proj, conv_w, doc_len, starts, out, mixed, key_t, query_t, m1, m2, tail,
-           prior, valid_cols, causal, tail_rows, halo, local, from_plane, total, from_z,
-           carry_out, carried, norm, acc, phi_q, halo_sem, a_send, a_recv, b_send, b_recv,
-           c_send, c_recv):
+def kernel(n, proj_hbm, conv_hbm, doc_len, starts, out, proj, conv_w, mixed, key_t, query_t, m1, m2, tail,
+           prior, causal, tail_rows, halo, local, from_plane, total, from_z,
+           carry_out, carried, acc, phi_q, halo_sem, a_send, a_recv, b_send, b_recv,
+           c_send, c_recv, load_sem):
+    loads = [pltpu.make_async_copy(proj_hbm, proj, load_sem.at[0]),
+             pltpu.make_async_copy(conv_hbm, conv_w, load_sem.at[1])]
+    for load in loads:
+        load.start()
     length = proj.shape[0]
     channels = proj.shape[1]
     me = lax.axis_index("seq")
@@ -80,6 +84,9 @@
     order = lax.broadcasted_iota(jnp.int32, (16, length), 0)
     last_two = (token == count - 2 + order) & (order < 2)
     pick_last = jnp.where(last_two, 1.0, 0.0).astype(BF16)
+
+    for load in loads:
+        load.wait()
 
     def pick(tile, _):
         at = lanes(tile * 4, 512)
@@ -136,7 +143,9 @@
         part = slice(i * 128, i * 128 + 128)
         u = lax.broadcasted_iota(jnp.int32, (length, 128), 1) + i * 128
         same = (start_col == start_row[:, part]) & (u <= slot_col) & valid_col
-        causal[:, part] = jnp.where(same, 1.0, 0.0).astype(BF16)
+        same = jnp.where(same, 1.0, 0.0).astype(BF16)
+        causal[:, i * 256:i * 256 + 128] = same
+        causal[:, i * 256 + 128:i * 256 + 256] = same
 
     def conv(tile, _):
         at = lanes(tile)
@@ -178,24 +187,20 @@
         pair = chunk * PER + pp
         v = values_at(pair) * tail[...]
         keys = key_t[pl.ds(pl.multiple_of(pair * 32, 32), 32), :]
-        s_even = jnp.dot(features(keys[:16], 1.0, 1.0).astype(BF16),
-                         jnp.where(low, v, tail[...]), preferred_element_type=F32)
-        s_odd = jnp.dot(features(keys[16:], 1.0, 1.0).astype(BF16),
-                        jnp.where(low, tail[...], v), preferred_element_type=F32)
-        local[d, :, lanes(pp)] = jnp.where(low, s_even, s_odd).astype(BF16)
-        norm[...] = jnp.where(lane == pp + 64, s_even, jnp.where(lane == pp, s_odd, norm[...]))
+        phi = jnp.concatenate(
+            [features(keys[:16], 1.0, 1.0), features(keys[16:], 1.0, 1.0)], axis=0).astype(BF16)
+        both = jnp.dot(phi, jnp.concatenate([v, tail[...]], axis=1), preferred_element_type=F32)
+        local[d, :, lanes(pp)] = jnp.where(low, both[:ROWS, :128], both[ROWS:, :128]).astype(BF16)
+        return jnp.where(lane == pp + 64, both[:ROWS, 128:],
+                         jnp.where(lane == pp, both[ROWS:, 128:], 0.0))
 
     a_copies = {}
     for d in (1, 2, 3, 0):
         chunk = (j + d) % PLANE
-        norm[...] = jnp.zeros_like(norm)
-
-        def step(pp, _, d=d, chunk=chunk):
-            state_pair(d, chunk, pp)
-            return 0
-
-        lax.fori_loop(0, PER, step, 0)
-        local[d, :, PER * 128:] = norm[...].astype(BF16)
+        norm = jnp.zeros((ROWS, 128), F32)
+        for pp in range(PER):
+            norm = norm + state_pair(d, chunk, pp)
+        local[d, :, PER * 128:] = norm.astype(BF16)
         if d:
             a_copies[d] = pltpu.make_async_remote_copy(
                 src_ref=local.at[d], dst_ref=from_plane.at[d], send_sem=a_send.at[d],
@@ -241,25 +246,36 @@
     lax.fori_loop(HEADS // 2, HEADS, query_features, 0)
 
     key_row = lax.broadcasted_iota(jnp.int32, (128, 1), 0) // FEAT
-    half = 256
+    blocks = length // 128
+
     def attend(pair, _):
         tile = pair // 4
         v = values_at(pair)
         q = mixed[:, lanes(tile)]
         keys = key_t[lanes(tile), :]
-        one = jnp.ones_like(v)
-        for side in range(2):
-            here = (pair % 4) * 2 + side
-            k = jnp.where(key_row == here, keys, 0.0).astype(BF16)
-            va = jnp.where(low, v, one) if side == 0 else jnp.where(low, one, v)
-            for lo, hi in ((0, half), (half, length)):
-                s = jnp.dot(q[lo:hi], k[:, :hi], preferred_element_type=F32) + 1.0
-                w = (s * s + 1.0).astype(BF16) * causal[lo:hi, :hi]
-                acc[pair * 2 + side, lo:hi, :] = jnp.dot(
-                    w, va[:hi], preferred_element_type=F32)
-        return 0
-
-    lax.fori_loop(0, PAIRS * 5 // 8, attend, 0)
+        here = (pair % 4) * 2
+        k_even = jnp.where(key_row == here, keys, 0.0).astype(BF16)
+        k_odd = jnp.where(key_row == here + 1, keys, 0.0).astype(BF16)
+        one, nil = jnp.ones((128, 128), BF16), jnp.zeros((128, 128), BF16)
+        sums = []
+        for b in range(blocks):
+            part = slice(b * 128, b * 128 + 128)
+            k = jnp.concatenate([k_even[:, part], k_odd[:, part]], axis=1)
+            s = jnp.dot(q[b * 128:], k, preferred_element_type=F32) + 1.0
+            w = (s * s + 1.0).astype(BF16) * causal[b * 128:, b * 256:b * 256 + 256]
+            va = jnp.concatenate([
+                jnp.concatenate([jnp.where(low, v[part], one), nil], axis=1),
+                jnp.concatenate([nil, jnp.where(low, one, v[part])], axis=1)], axis=0)
+            sums.append(jnp.dot(w, va, preferred_element_type=F32))
+        for b in range(blocks):
+            rows = slice(b * 128, b * 128 + 128)
+            whole = sums[0][rows]
+            for e in range(1, b + 1):
+                whole = whole + sums[e][(b - e) * 128:(b - e) * 128 + 128]
+            acc[pair, rows, :] = whole
+        return 0
+
+    lax.fori_loop(0, PAIRS * 5 // 8, attend, 0, unroll=2)
 
     for k in (1, 2):
         pl.when(z >= k)(b_copies[k - 1].wait_recv)
@@ -284,34 +300,33 @@
         else:
             carried[0] = state.astype(BF16)
 
-    lax.fori_loop(PAIRS * 5 // 8, PAIRS, attend, 0)
-
-    from_row = lax.broadcasted_iota(jnp.int32, (128, 256), 0)
-    to_col = lax.broadcasted_iota(jnp.int32, (128, 256), 1)
+    lax.fori_loop(PAIRS * 5 // 8, PAIRS, attend, 0, unroll=2)
+
+    from_row = lax.broadcasted_iota(jnp.int32, (128, PER * 256), 0)
+    to_col = lax.broadcasted_iota(jnp.int32, (128, PER * 256), 1)
+    spread = jnp.where(
+        from_row == to_col // 256 + jnp.where(to_col % 256 < 128, 64, 0), 1.0, 0.0).astype(BF16)
     pad = jnp.zeros((256 - ROWS, 128), BF16)
     for d in range(PLANE):
         if d:
             c_copies[d].wait_recv()
         chunk = (j - d + PLANE) % PLANE
 
-        def finish(pp, _, d=d, chunk=chunk):
+        norms = jnp.dot(carried[d, :, PER * 128:], spread, preferred_element_type=F32).astype(BF16)
+        for pp in range(PER):
             pair = chunk * PER + pp
-            values = carried[d, :, lanes(pp)]
-            pick = ((from_row == pp + 64) & (to_col < 128)) | ((from_row == pp) & (to_col >= 128))
-            norms = jnp.dot(carried[d, :, PER * 128:], jnp.where(pick, 1.0, 0.0).astype(BF16),
-                            preferred_element_type=F32).astype(BF16)
-            s_even = jnp.concatenate([jnp.where(low, values, norms[:, :128]), pad], axis=0)
-            s_odd = jnp.concatenate([jnp.where(low, norms[:, 128:], values), pad], axis=0)
-            even = acc[pair * 2] + jnp.dot(phi_q[pair * 2], s_even, preferred_element_type=F32)
-            odd = acc[pair * 2 + 1] + jnp.dot(phi_q[pair * 2 + 1], s_odd, preferred_element_type=F32)
+            values = carried[d, :, pp * 128:pp * 128 + 128]
+            norm = norms[:, pp * 256:pp * 256 + 256]
+            s_even = jnp.concatenate([jnp.where(low, values, norm[:, :128]), pad], axis=0)
+            s_odd = jnp.concatenate([jnp.where(low, norm[:, 128:], values), pad], axis=0)
+            mine = acc[pair]
+            even = mine[:, :128] + jnp.dot(phi_q[pair * 2], s_even, preferred_element_type=F32)
+            odd = mine[:, 128:] + jnp.dot(phi_q[pair * 2 + 1], s_odd, preferred_element_type=F32)
             numer = jnp.where(low, even, odd)
             denom = pltpu.roll(jnp.where(low, odd, even), 64, 1)
             good = denom != 0.0
             result = jnp.where(good, numer / jnp.where(good, denom, 1.0), 0.0)
             out[:, lanes(pair)] = result.astype(BF16)
-            return 0
-
-        lax.fori_loop(0, PER, finish, 0)
 
     pl.when(me < n - 1)(halo_copy.wait_send)
     for d in range(1, PLANE):
@@ -330,9 +345,11 @@
     return pl.pallas_call(
         functools.partial(kernel, n),
         out_shape=jax.ShapeDtypeStruct((length, HEADS * HEAD_DIM), BF16),
-        in_specs=[vmem, vmem, smem, smem],
+        in_specs=[pl.BlockSpec(memory_space=pl.ANY)] * 2 + [smem, smem],
         out_specs=vmem,
         scratch_shapes=[
+            pltpu.VMEM((length, channels), BF16),
+            pltpu.VMEM(conv_weight.shape, F32),
             pltpu.VMEM((length, channels), BF16),
             pltpu.VMEM((KEYS, length), F32),
             pltpu.VMEM((KEYS, length), F32),
@@ -340,8 +357,7 @@
             pltpu.VMEM((length, 128), F32),
             pltpu.VMEM((length, 128), BF16),
             pltpu.VMEM((8, length), F32),
-            pltpu.VMEM((8, 128), F32),
-            pltpu.VMEM((length, length), BF16),
+            pltpu.VMEM((length, 2 * length), BF16),
             pltpu.VMEM((16, channels), BF16),
             pltpu.VMEM((16, channels), BF16),
             pltpu.VMEM((PLANE,) + state, BF16),
@@ -350,8 +366,7 @@
             pltpu.VMEM((2,) + state, BF16),
             pltpu.VMEM((PLANE,) + state, BF16),
             pltpu.VMEM((PLANE,) + state, BF16),
-            pltpu.VMEM((ROWS, 128), F32),
-            pltpu.VMEM((HEADS, length, 128), F32),
+            pltpu.VMEM((PAIRS, length, 256), F32),
             pltpu.VMEM((HEADS, length, 256), BF16),
             pltpu.SemaphoreType.DMA((2,)),
             pltpu.SemaphoreType.DMA((PLANE,)),
@@ -360,9 +375,10 @@
             pltpu.SemaphoreType.DMA((2,)),
             pltpu.SemaphoreType.DMA((PLANE,)),
             pltpu.SemaphoreType.DMA((PLANE,)),
+            pltpu.SemaphoreType.DMA((2,)),
         ],
         compiler_params=pltpu.CompilerParams(
-            collective_id=0, has_side_effects=True, vmem_limit_bytes=48 * 1024 * 1024),
+            collective_id=0, has_side_effects=True, vmem_limit_bytes=60 * 1024 * 1024),
     )(projected, conv_weight, doc_lengths, load_starts)
 
 

time: 50.1 us -> 46.1 us (0.920)
  local copies, waits for them, and re-layouts: 4.92 us -> 2.73 us
  Pallas kernels: 44.9 us -> 43.2 us
    unnamed x9 -> x1, local copies, waits for them, and re-layouts: 4.92 us -> 2.73 us
    pallas_call x1, Pallas kernels: 44.9 us -> 43.2 us  [per_device(): pl.pallas_call(functools.partial(kernel, n), out_shape=jax.ShapeDtypeStru...]
where the time goes in v2:
time: 46.1 us; the launch traced here: 45.9 us
  Pallas kernels  43.2 us (94%)
  local copies, waits for them, and re-layouts  2.73 us (6%)
    pallas_call x1, Pallas kernels, per_device(): pl.pallas_call(functools.partial(kernel, n), out_shape=jax.ShapeDtypeStru...  43.2 us
    unnamed x1, local copies, waits for them, and re-layouts  2.73 us

profile of v2, /device:TPU:27, one launch (start us, length us, event | category | flops | bytes accessed | tf_op | source)
XLA Modules:
  0.0 45.9 jit_solution(16703206620982970874)
XLA Ops:
  0.0 43.2 %shard_map.46 = bf16[384,2048]{1,0:T(8,128)(2,1)} custom-call(bf16[384,3072]{1,0:T(8,128)(2,1)} %proj_hbm.1, f32[3,3072]{1,0:T(4,128)} %conv_hbm.1, s32[32]{0:T(128)} %doc_len.1, s32[16]{0:T(128)} %starts.1), custom_call_target="tpu_custom_call" | custom-call | tf_op jit(solution)/shard_map/pallas_call | solution.py:345
  43.2 2.7 %copy.6 = bf16[384,2048]{1,0:T(8,128)(2,1)} copy(bf16[384,2048]{1,0:T(8,128)(2,1)} %shard_map.46) | data formatting | bytes 3145728

commit v3 on v2

--- a/solution.py
+++ b/solution.py
@@ -15,6 +15,7 @@
 KEYS = HEADS * FEAT
 PAIRS = HEADS // 2
 PER = PAIRS // PLANE
+PARTS = 2
 ROWS = 160
 MESH = pl.DeviceIdType.MESH
 F32 = jnp.float32
@@ -183,29 +184,40 @@
     def values_at(pair):
         return mixed[:, lanes(pair + 2 * KEYS // 128)]
 
-    def state_pair(d, chunk, pp):
-        pair = chunk * PER + pp
-        v = values_at(pair) * tail[...]
-        keys = key_t[pl.ds(pl.multiple_of(pair * 32, 32), 32), :]
-        phi = jnp.concatenate(
-            [features(keys[:16], 1.0, 1.0), features(keys[16:], 1.0, 1.0)], axis=0).astype(BF16)
-        both = jnp.dot(phi, jnp.concatenate([v, tail[...]], axis=1), preferred_element_type=F32)
-        local[d, :, lanes(pp)] = jnp.where(low, both[:ROWS, :128], both[ROWS:, :128]).astype(BF16)
-        return jnp.where(lane == pp + 64, both[:ROWS, 128:],
-                         jnp.where(lane == pp, both[ROWS:, 128:], 0.0))
+    row16_part = lax.broadcasted_iota(jnp.int32, (16, 256), 0)
+
+    def state_part(d, chunk, h):
+        ends = jnp.zeros((16, 256), F32)
+        for i in range(PER // PARTS):
+            pair = chunk * PER + h * (PER // PARTS) + i
+            v = values_at(pair) * tail[...]
+            keys = key_t[pl.ds(pl.multiple_of(pair * 32, 32), 32), :]
+            phi = jnp.concatenate(
+                [features(keys[:16], 1.0, 1.0), features(keys[16:], 1.0, 1.0)],
+                axis=0).astype(BF16)
+            both = jnp.dot(phi, jnp.concatenate([v, tail[...]], axis=1),
+                           preferred_element_type=F32)
+            local[d, h, :, i * 128:i * 128 + 128] = jnp.where(
+                low, both[:ROWS, :128], both[ROWS:, :128]).astype(BF16)
+            for side in range(2):
+                column = both[side * ROWS:side * ROWS + ROWS, 128:]
+                turned = jnp.concatenate(
+                    [column, jnp.zeros((256 - ROWS, 128), F32)], axis=0).T[:1]
+                ends = ends + jnp.where(row16_part == 9 + 2 * i + side, turned, 0.0)
+        last_rows = local[d, h, ROWS - 16:, :].astype(F32)
+        local[d, h, ROWS - 16:, :] = jnp.where(row16_part < 9, last_rows, ends).astype(BF16)
 
     a_copies = {}
-    for d in (1, 2, 3, 0):
-        chunk = (j + d) % PLANE
-        norm = jnp.zeros((ROWS, 128), F32)
-        for pp in range(PER):
-            norm = norm + state_pair(d, chunk, pp)
-        local[d, :, PER * 128:] = norm.astype(BF16)
-        if d:
-            a_copies[d] = pltpu.make_async_remote_copy(
-                src_ref=local.at[d], dst_ref=from_plane.at[d], send_sem=a_send.at[d],
-                recv_sem=a_recv.at[d], device_id={"seq": base + chunk}, device_id_type=MESH)
-            a_copies[d].start()
+    for h in range(PARTS):
+        for d in (1, 2, 3, 0):
+            chunk = (j + d) % PLANE
+            state_part(d, chunk, h)
+            if d:
+                a_copies[d, h] = pltpu.make_async_remote_copy(
+                    src_ref=local.at[d, h], dst_ref=from_plane.at[d, h],
+                    send_sem=a_send.at[d, h], recv_sem=a_recv.at[d, h],
+                    device_id={"seq": base + chunk}, device_id_type=MESH)
+                a_copies[d, h].start()
 
     def turn_queries(tile, _):
         at = lanes(tile)
@@ -223,27 +235,28 @@
         phi_q[head] = phi.astype(BF16).T
         return 0
 
-    lax.fori_loop(0, HEADS // 2, query_features, 0)
-
-    def gathered(d):
-        return local[0] if d == 0 else from_plane[d]
-
-    for d in range(1, PLANE):
-        a_copies[d].wait_recv()
-    total_sum = jnp.zeros(total.shape, F32)
-    for d in range(PLANE):
-        source = (j - d + PLANE) % PLANE
-        keep = jnp.where(opens[PLANE] < start_of(base + source + 1), 1.0, 0.0)
-        total_sum = total_sum + gathered(d).astype(F32) * keep
-    total[...] = total_sum.astype(BF16)
-    b_copies = []
-    for k in (1, 2):
-        b_copies.append(pltpu.make_async_remote_copy(
-            src_ref=total, dst_ref=from_z.at[k - 1], send_sem=b_send.at[k - 1],
-            recv_sem=b_recv.at[k - 1], device_id={"seq": me + k * PLANE}, device_id_type=MESH))
-        pl.when(z < planes - k)(b_copies[-1].start)
-
-    lax.fori_loop(HEADS // 2, HEADS, query_features, 0)
+    def gathered(d, h):
+        return local[0, h] if d == 0 else from_plane[d, h]
+
+    b_copies = {}
+    for h in range(PARTS):
+        lax.fori_loop(h * 8, h * 8 + 8, query_features, 0)
+        for d in range(1, PLANE):
+            a_copies[d, h].wait_recv()
+        total_sum = jnp.zeros((ROWS, 256), F32)
+        for d in range(PLANE):
+            source = (j - d + PLANE) % PLANE
+            keep = jnp.where(opens[PLANE] < start_of(base + source + 1), 1.0, 0.0)
+            total_sum = total_sum + gathered(d, h).astype(F32) * keep
+        total[h] = total_sum.astype(BF16)
+        for k in (1, 2):
+            b_copies[k, h] = pltpu.make_async_remote_copy(
+                src_ref=total.at[h], dst_ref=from_z.at[k - 1, h], send_sem=b_send.at[k - 1, h],
+                recv_sem=b_recv.at[k - 1, h], device_id={"seq": me + k * PLANE},
+                device_id_type=MESH)
+            pl.when(z < planes - k)(b_copies[k, h].start)
+
+    lax.fori_loop(16, HEADS, query_features, 0)
 
     key_row = lax.broadcasted_iota(jnp.int32, (128, 1), 0) // FEAT
     blocks = length // 128
@@ -275,48 +288,48 @@
             acc[pair, rows, :] = whole
         return 0
 
-    lax.fori_loop(0, PAIRS * 5 // 8, attend, 0, unroll=2)
-
-    for k in (1, 2):
-        pl.when(z >= k)(b_copies[k - 1].wait_recv)
     c_copies = {}
-    for d in (1, 2, 3, 0):
-        to = (j + d) % PLANE
-        open_at = opens[0]
-        for i in range(1, PLANE):
-            open_at = jnp.where(to == i, opens[i], open_at)
-        state = from_z[0].astype(F32) * jnp.where(open_at < edge[PLANE], 1.0, 0.0)
-        state = state + from_z[1].astype(F32) * jnp.where(open_at < edge[0], 1.0, 0.0)
-        for e in range(PLANE):
-            source = (j - e + PLANE) % PLANE
-            keep = (source < to) & (open_at < start_of(base + source + 1))
-            state = state + gathered(e).astype(F32) * jnp.where(keep, 1.0, 0.0)
+    for h in range(PARTS):
+        lax.fori_loop(h * 4, h * 4 + 4, attend, 0, unroll=2)
+        for k in (1, 2):
+            pl.when(z >= k)(b_copies[k, h].wait_recv)
+        for d in (1, 2, 3, 0):
+            to = (j + d) % PLANE
+            open_at = opens[0]
+            for i in range(1, PLANE):
+                open_at = jnp.where(to == i, opens[i], open_at)
+            state = from_z[0, h].astype(F32) * jnp.where(open_at < edge[PLANE], 1.0, 0.0)
+            state = state + from_z[1, h].astype(F32) * jnp.where(open_at < edge[0], 1.0, 0.0)
+            for e in range(PLANE):
+                source = (j - e + PLANE) % PLANE
+                keep = (source < to) & (open_at < start_of(base + source + 1))
+                state = state + gathered(e, h).astype(F32) * jnp.where(keep, 1.0, 0.0)
+            if d:
+                carry_out[d, h] = state.astype(BF16)
+                c_copies[d, h] = pltpu.make_async_remote_copy(
+                    src_ref=carry_out.at[d, h], dst_ref=carried.at[d, h],
+                    send_sem=c_send.at[d, h], recv_sem=c_recv.at[d, h],
+                    device_id={"seq": base + to}, device_id_type=MESH)
+                c_copies[d, h].start()
+            else:
+                carried[0, h] = state.astype(BF16)
+
+    lax.fori_loop(PAIRS // 2, PAIRS, attend, 0, unroll=2)
+
+    from_row = lax.broadcasted_iota(jnp.int32, (16, 512), 0)
+    to_col = lax.broadcasted_iota(jnp.int32, (16, 512), 1)
+    spread = jnp.where(from_row == 9 + to_col // 128, 1.0, 0.0).astype(BF16)
+    pad = jnp.zeros((256 - ROWS, 128), BF16)
+    for h, d in [(h, d) for h in range(PARTS) for d in range(PLANE)]:
         if d:
-            carry_out[d] = state.astype(BF16)
-            c_copies[d] = pltpu.make_async_remote_copy(
-                src_ref=carry_out.at[d], dst_ref=carried.at[d], send_sem=c_send.at[d],
-                recv_sem=c_recv.at[d], device_id={"seq": base + to}, device_id_type=MESH)
-            c_copies[d].start()
-        else:
-            carried[0] = state.astype(BF16)
-
-    lax.fori_loop(PAIRS * 5 // 8, PAIRS, attend, 0, unroll=2)
-
-    from_row = lax.broadcasted_iota(jnp.int32, (128, PER * 256), 0)
-    to_col = lax.broadcasted_iota(jnp.int32, (128, PER * 256), 1)
-    spread = jnp.where(
-        from_row == to_col // 256 + jnp.where(to_col % 256 < 128, 64, 0), 1.0, 0.0).astype(BF16)
-    pad = jnp.zeros((256 - ROWS, 128), BF16)
-    for d in range(PLANE):
-        if d:
-            c_copies[d].wait_recv()
+            c_copies[d, h].wait_recv()
         chunk = (j - d + PLANE) % PLANE
-
-        norms = jnp.dot(carried[d, :, PER * 128:], spread, preferred_element_type=F32).astype(BF16)
-        for pp in range(PER):
-            pair = chunk * PER + pp
-            values = carried[d, :, pp * 128:pp * 128 + 128]
-            norm = norms[:, pp * 256:pp * 256 + 256]
+        norms = lax.dot_general(carried[d, h, ROWS - 16:, :], spread, (((0,), (0,)), ((), ())),
+                                preferred_element_type=F32).astype(BF16)[:ROWS]
+        for i in range(PER // PARTS):
+            pair = chunk * PER + h * (PER // PARTS) + i
+            values = carried[d, h, :, i * 128:i * 128 + 128]
+            norm = norms[:, i * 256:i * 256 + 256]
             s_even = jnp.concatenate([jnp.where(low, values, norm[:, :128]), pad], axis=0)
             s_odd = jnp.concatenate([jnp.where(low, norm[:, 128:], values), pad], axis=0)
             mine = acc[pair]
@@ -329,17 +342,18 @@
             out[:, lanes(pair)] = result.astype(BF16)
 
     pl.when(me < n - 1)(halo_copy.wait_send)
-    for d in range(1, PLANE):
-        a_copies[d].wait_send()
-        c_copies[d].wait_send()
-    for k in (1, 2):
-        pl.when(z < planes - k)(b_copies[k - 1].wait_send)
+    for h in range(PARTS):
+        for d in range(1, PLANE):
+            a_copies[d, h].wait_send()
+            c_copies[d, h].wait_send()
+        for k in (1, 2):
+            pl.when(z < planes - k)(b_copies[k, h].wait_send)
 
 
 def per_device(projected, conv_weight, doc_lengths, load_starts):
     n = lax.axis_size("seq")
     length, channels = projected.shape
-    state = (ROWS, (PER + 1) * 128)
+    state = (PARTS, ROWS, PER // PARTS * 128)
     vmem = pl.BlockSpec(memory_space=pltpu.VMEM)
     smem = pl.BlockSpec(memory_space=pltpu.SMEM)
     return pl.pallas_call(
@@ -369,12 +383,12 @@
             pltpu.VMEM((PAIRS, length, 256), F32),
             pltpu.VMEM((HEADS, length, 256), BF16),
             pltpu.SemaphoreType.DMA((2,)),
-            pltpu.SemaphoreType.DMA((PLANE,)),
-            pltpu.SemaphoreType.DMA((PLANE,)),
-            pltpu.SemaphoreType.DMA((2,)),
-            pltpu.SemaphoreType.DMA((2,)),
-            pltpu.SemaphoreType.DMA((PLANE,)),
-            pltpu.SemaphoreType.DMA((PLANE,)),
+            pltpu.SemaphoreType.DMA((PLANE, PARTS)),
+            pltpu.SemaphoreType.DMA((PLANE, PARTS)),
+            pltpu.SemaphoreType.DMA((2, PARTS)),
+            pltpu.SemaphoreType.DMA((2, PARTS)),
+            pltpu.SemaphoreType.DMA((PLANE, PARTS)),
+            pltpu.SemaphoreType.DMA((PLANE, PARTS)),
             pltpu.SemaphoreType.DMA((2,)),
         ],
         compiler_params=pltpu.CompilerParams(

time: 46.1 us -> 37.2 us (0.81)
  Pallas kernels: 43.2 us -> 34.3 us
    pallas_call x1, Pallas kernels: 43.2 us -> 34.3 us  [per_device(): pl.pallas_call(functools.partial(kernel, n), out_shape=jax.ShapeDtypeStru...]
where the time goes in v3:
time: 37.2 us; the launch traced here: 37 us
  Pallas kernels  34.3 us (92%)
  local copies, waits for them, and re-layouts  2.73 us (7%)
    pallas_call x1, Pallas kernels, per_device(): pl.pallas_call(functools.partial(kernel, n), out_shape=jax.ShapeDtypeStru...  34.3 us
    unnamed x1, local copies, waits for them, and re-layouts  2.73 us

profile of v3, /device:TPU:27, one launch (start us, length us, event | category | flops | bytes accessed | tf_op | source)
XLA Modules:
  0.0 37.0 jit_solution(7214053308736461261)
XLA Ops:
  0.0 34.3 %shard_map.46 = bf16[384,2048]{1,0:T(8,128)(2,1)} custom-call(bf16[384,3072]{1,0:T(8,128)(2,1)} %proj_hbm.1, f32[3,3072]{1,0:T(4,128)} %conv_hbm.1, s32[32]{0:T(128)} %doc_len.1, s32[16]{0:T(128)} %starts.1), custom_call_target="tpu_custom_call" | custom-call | tf_op jit(solution)/shard_map/pallas_call | solution.py:359
  34.3 2.7 %copy.6 = bf16[384,2048]{1,0:T(8,128)(2,1)} copy(bf16[384,2048]{1,0:T(8,128)(2,1)} %shard_map.46) | data formatting | bytes 3145728
